TPU v7x, 512 devices: a whole 4x8x8 slice. The times are simulated.
512 devices in a mesh: lon: 64 (over y, z_hi, core), lat: 8 (over x, z_lo).
Axes of the slice: x: 4, y: 8, z: 8 (z_hi: 4, z_lo: 2; z = z_hi * 2 + z_lo), core: 2. Of those that a mesh axis runs over, the one named last changes fastest.
Arguments:
- state_field: float32 [48, 2048, 1024], P(None, 'lon', 'lat'), may hold values from -6 to 6
- weight_bank: float32 [9, 48, 48], replicated, may hold values from -0.3125 to 0.3125
- cotangent: float32 [48, 2048, 1024], P(None, 'lon', 'lat'), may hold values from -6 to 6
Outputs:
- response: float32 [48, 2048, 1024], P(None, 'lon', 'lat')
- grad_field: float32 [48, 2048, 1024], P(None, 'lon', 'lat')
- grad_weight: float32 [9, 48, 48], replicated
All inputs are finite; a program needn't handle non-finite values.
Results may differ from a plain program's by a relative error of at most 0.0003.
Values sent between devices are 32-bit elements; how exact they have to be, the bound alone decides.
A program may use at most 64 MiB of HBM per device.

v0:
```python
import math

import jax
import jax.numpy as jnp
from jax import lax
from jax.sharding import PartitionSpec as P


def padded(cells, sides, width, closed):
    for axis, dim in sides:
        count = lax.axis_size(axis)
        ends = count if closed else count - 1
        head = lax.slice_in_dim(cells, 0, width, axis=dim)
        tail = lax.slice_in_dim(cells, cells.shape[dim] - width, cells.shape[dim], axis=dim)
        cells = jnp.concatenate(
            [
                lax.ppermute(tail, axis, [(i, (i + 1) % count) for i in range(ends)]),
                cells,
                lax.ppermute(head, axis, [((i + 1) % count, i) for i in range(ends)]),
            ],
            axis=dim,
        )
    return cells


def passed_along(value, axis, steps):
    count = lax.axis_size(axis)
    pairs = [(source, (source + steps) % count) for source in range(count)]
    return lax.ppermute(value, axis, pairs)


def conv_valid(grid, kernel):
    return lax.conv_general_dilated(
        grid[None], kernel, (1, 1), "VALID", precision=lax.Precision.HIGHEST
    )[0]


def extend_grid(stacked, is_north, is_south):
    widened = padded(stacked, (("lon", 1),), 1, True)
    banded = padded(widened, (("lat", 2),), 1, False)
    pole_rows = jnp.concatenate([widened[:, :, :1], widened[:, :, -1:]], axis=2)
    far_rows = passed_along(pole_rows, "lon", lax.axis_size("lon") // 2)
    first_row = jnp.where(is_north, far_rows[:, :, 0:1], banded[:, :, 0:1])
    final_row = jnp.where(is_south, far_rows[:, :, 1:2], banded[:, :, -1:])
    return jnp.concatenate([first_row, banded[:, :, 1:-1], final_row], axis=2)


def body(state_field, weight_bank, cotangent):
    channels = state_field.shape[0]
    cols_here = state_field.shape[1]
    rows_here = state_field.shape[2]
    grid_weights = weight_bank.reshape(3, 3, channels, channels)
    forward_kernel = grid_weights.transpose(2, 3, 1, 0)
    adjoint_kernel = jnp.flip(grid_weights, (0, 1)).transpose(3, 2, 1, 0)
    is_north = lax.axis_index("lat") == 0
    is_south = lax.axis_index("lat") == lax.axis_size("lat") - 1
    extended = extend_grid(jnp.concatenate([state_field, cotangent], axis=0), is_north, is_south)
    field_ext = extended[:channels]
    grad_ext = extended[channels:]
    response = conv_valid(field_ext, forward_kernel)
    inner_grad = jnp.concatenate(
        [
            jnp.where(is_north, 0.0, grad_ext[:, :, :1]),
            grad_ext[:, :, 1:-1],
            jnp.where(is_south, 0.0, grad_ext[:, :, -1:]),
        ],
        axis=2,
    )
    grad_field = conv_valid(inner_grad, adjoint_kernel)
    north_term = conv_valid(grad_ext[:, :, :1], adjoint_kernel[:, :, :, 2:3])
    south_term = conv_valid(grad_ext[:, :, -1:], adjoint_kernel[:, :, :, 0:1])
    grad_field = grad_field.at[:, :, :1].add(jnp.where(is_north, north_term, 0.0))
    grad_field = grad_field.at[:, :, -1:].add(jnp.where(is_south, south_term, 0.0))
    tap_terms = []
    for tap_index in range(9):
        row_off = tap_index // 3
        col_off = tap_index % 3
        window = field_ext[:, col_off : col_off + cols_here, row_off : row_off + rows_here]
        tap_terms.append(
            jnp.einsum("ohw,chw->oc", cotangent, window, precision=lax.Precision.HIGHEST)
        )
    local_weight = jnp.stack(tap_terms, axis=0)
    summed = lax.psum(local_weight, ("lon", "lat"))
    total_cells = rows_here * lax.axis_size("lat") * cols_here * lax.axis_size("lon")
    grad_weight = summed * (1.0 / math.sqrt(total_cells))
    return (response, grad_field, grad_weight)


def solution(mesh):
    in_specs = (P(None, "lon", "lat"), P(), P(None, "lon", "lat"))
    out_specs = (P(None, "lon", "lat"), P(None, "lon", "lat"), P())
    return jax.shard_map(body, mesh=mesh, in_specs=in_specs, out_specs=out_specs, check_vma=False)
```

profile of v0, /device:TPU:1, one launch (start us, length us, event | category | flops | bytes accessed | tf_op | source)
XLA Modules:
  0.0 360.8 jit_solution(10127913144265419421)
XLA Ops:
  7.2 0.0 copy-start.1
  7.2 0.0 all-reduce.2.cloned.1.call-start
  7.2 1.8 copy.34
  9.0 0.0 copy-done.1
  9.1 2.0 copy.33
  11.1 0.0 copy-start.3
  11.1 1.0 pad_maximum_fusion.26
  12.1 7.2 %collective-permute-start = (f32[96,1,128]{0,2,1:T(8,128)S(1)}, f32[96,1,128]{0,2,1:T(8,128)S(1)}, u32[]{:S(2)}, u32[]{:S(2)}) collective-permute-start(f32[96,1,128]{0,2,1:T(8,128)S(1)} %get-tuple-element.39), channel_id=1, source_target_pairs={{0,8},{8,16},{16,24},{24,32},{32,40},{40,48},{48,56},{56,64},{64,7... | collective-permute-start | bytes 147464 | tf_op jit(solution)/shard_map/ppermute | solution.py:17
  19.3 3.5 collective-permute-start.1
  22.8 0.0 copy-done.3
  22.8 0.1 copy.44
  22.9 0.0 collective-permute-done
  22.9 2.8 collective-permute-done.1
  25.8 1.1 pad_maximum_fusion.28
  26.9 4.3 %collective-permute-start.3 = (f32[96,34,1]{0,2,1:T(1,128)S(1)}, f32[96,34,1]{0,2,1:T(1,128)S(1)}, u32[]{:S(2)}, u32[]{:S(2)}) collective-permute-start(f32[96,34,1]{0,2,1:T(1,128)S(1)} %get-tuple-element.37), channel_id=1, source_target_pairs={{0,1},{1,2},{2,3},{3,4},{4,5},{5,6},{6,7},{8,9},{9,10},{10,11},{11... | collective-permute-start | bytes 39176 | tf_op jit(solution)/shard_map/ppermute | solution.py:17
  31.2 1.3 collective-permute-start.4
  32.5 7.2 %collective-permute-start.2 = (f32[96,34,2]{0,2,1:T(2,128)S(1)}, f32[96,34,2]{0,2,1:T(2,128)S(1)}, u32[]{:S(2)}, u32[]{:S(2)}) collective-permute-start(f32[96,34,2]{0,2,1:T(2,128)S(1)} %pad_maximum_fusion.27), channel_id=1, source_target_pairs={{0,256},{8,264},{16,272},{24,280},{32,288},{40,296},{48,304},{56,3... | collective-permute-start | bytes 78344 | tf_op jit(solution)/shard_map/ppermute | solution.py:29
  39.7 0.0 collective-permute-done.3
  39.7 0.0 collective-permute-done.4
  39.7 1.5 collective-permute-done.2
  41.3 0.1 broadcast_select_fusion
  41.4 5.3 %pad_maximum_fusion.8 = (f32[96,34,129]{0,2,1:T(8,128)S(1)}, f32[96,34,129]{0,2,1:T(8,128)S(1)}) fusion(f32[96,34,1]{0,2,1:T(1,128)S(1)} %get-tuple-element.44, f32[96,1,128]{0,2,1:T(8,128)S(1)} %collective-permute-done.1, f32[48,32,128]{0,2,1:T(8,128)S(1)} %copy.34, f32[48,32,128]{0,2,1:T(8,128)} %copy.33, f32[96,1,128]{0,2,1:T(8,128)S(1)} %collective-permute-done, ...), kind=kLoop, calls=%fused_computation.24 | loop fusion | flops 3368448 | bytes 5065728 | tf_op jit(solution)/shard_map/concatenate | solution.py:45
  46.7 3.4 fusion.43
  50.2 3.4 fusion.49
  53.6 0.0 copy-start
  53.6 3.4 fusion.55
  57.0 0.0 copy-done
  57.0 4.3 %fusion.59 = f32[9,48,48]{1,2,0:T(8,128)S(1)} fusion(f32[9,48,48]{1,2,0:T(8,128)S(1)} %fusion.55, f32[48,32,128]{0,2,1:T(8,128)S(1)} %copy.34, f32[96,1,128]{0,2,1:T(8,128)S(1)} %collective-permute-done, f32[48,32,128]{0,2,1:T(8,128)S(1)} %copy-done), kind=kOutput, calls=%fused_computation.59 | convolution fusion | flops 113639424 | bytes 6381568 | tf_op jit(solution)/shard_map/ohw,chw->oc/dot_general | solution.py:80
  61.3 3.6 %fusion.80 = f32[9,48,48]{1,2,0:T(8,128)S(1)} fusion(f32[9,48,48]{1,2,0:T(8,128)S(1)} %fusion.59, f32[48,32,128]{0,2,1:T(8,128)S(1)} %copy.34, f32[48,32,128]{0,2,1:T(8,128)S(1)} %copy-done), kind=kOutput, calls=%fused_computation.69 | convolution fusion | flops 113246208 | bytes 4218880 | tf_op jit(solution)/shard_map/ohw,chw->oc/dot_general | solution.py:80
  64.9 4.1 %fusion.61 = f32[9,48,48]{1,2,0:T(8,128)S(1)} fusion(f32[9,48,48]{1,2,0:T(8,128)S(1)} %fusion.80, f32[48,32,128]{0,2,1:T(8,128)S(1)} %copy.34, f32[96,1,128]{0,2,1:T(8,128)S(1)} %collective-permute-done.1, f32[48,32,128]{0,2,1:T(8,128)S(1)} %copy-done), kind=kOutput, calls=%fused_computation.61 | convolution fusion | flops 113639424 | bytes 6381568 | tf_op jit(solution)/shard_map/ohw,chw->oc/dot_general | solution.py:80
  69.0 3.4 fusion.65
  72.5 3.9 %fusion.71 = f32[9,48,48]{1,2,0:T(8,128)S(1)} fusion(f32[9,48,48]{1,2,0:T(8,128)S(1)} %fusion.65, f32[48,32,128]{0,2,1:T(8,128)S(1)} %copy.34, f32[96,34,129]{0,2,1:T(8,128)S(1)} %get-tuple-element.33), kind=kOutput, calls=%fused_computation.65 | convolution fusion | flops 113246208 | bytes 4218880 | tf_op jit(solution)/shard_map/ohw,chw->oc/dot_general | solution.py:80
  76.4 3.4 fusion.77
  79.8 0.0 copy-start.2
  79.8 0.7 copy-done.2
  80.5 0.0 all-reduce.2.cloned.1.call-update
  80.5 6.5 %fusion.12 = (f32[48,34,1,130]{0,3,1,2:T(8,128)S(1)}, f32[48,34,1,130]{0,3,1,2:T(8,128)S(1)}) fusion(f32[96,1,128]{0,2,1:T(8,128)S(1)} %collective-permute-done.1, f32[96,1,128]{0,2,1:T(8,128)S(1)} %collective-permute-done, f32[48,32,128]{0,2,1:T(8,128)S(1)} %copy.34, f32[48,32,128]{0,2,1:T(8,128)} %copy.33, f32[48,34,1]{0,2,1:T(1,128)S(1)} %get-tuple-element.45, ...), kind=kLoop, calls=%fused_computation.14 | loop fusion | flops 2121600 | bytes 3407616 | tf_op jit(solution)/shard_map/broadcast_in_dim | solution.py:34
  87.1 0.2 pad.6
  87.2 0.0 copy-start.4
  87.2 0.2 copy.40
  87.4 0.5 copy-done.4
  87.9 17.2 %fusion.33 = f32[32,8,17,48]{3,1,2,0:T(8,128)S(1)} fusion(f32[3,3,48,48]{2,3,0,1:T(8,128)S(1)} %copy.44, f32[48,34,1,7,2]{0,3,4,1,2:T(8,128)S(1)} %slice.173, f32[48,34,1,8,17]{0,3,4,1,2:T(8,128)S(1)} %copy.40, pred[8,17]{0,1:T(8,128)(4,1)S(1)} %copy-done.4), kind=kOutput, calls=%fused_computation.47 | convolution fusion | flops 1083869952 | bytes 1897864 | tf_op jit(solution)/shard_map/conv_general_dilated | solution.py:33
  105.2 0.4 copy.42
  105.6 0.2 slice.174
  105.8 2.2 copy.84
  107.9 0.4 fusion.83
  108.4 0.2 pad.4
  108.6 0.2 copy.36
  108.8 9.6 %fusion.30 = f32[32,8,17,48]{3,1,2,0:T(8,128)S(1)} fusion(f32[3,3,48,48]{2,3,0,1:T(8,128)S(1)} %copy.44, f32[48,34,1,7,2]{0,3,4,1,2:T(8,128)S(1)} %slice.169, f32[48,34,1,8,17]{0,3,4,1,2:T(8,128)S(1)} %copy.36, pred[8,17]{0,1:T(8,128)(4,1)S(1)} %copy-done.4), kind=kOutput, calls=%fused_computation.46 | convolution fusion | flops 1083869952 | bytes 1897864 | tf_op jit(solution)/shard_map/conv_general_dilated | solution.py:33
  118.3 0.4 copy.38
  118.8 1.5 slice_bitcast_fusion
  120.3 0.4 fusion.82
  120.7 0.1 scatter-add.6
  120.9 0.1 scatter-add.9
  121.0 1.6 copy.69
  122.6 3.7 %copy.68 = f32[48,32,128]{2,1,0:T(8,128)} copy(f32[48,32,128]{0,1,2:T(8,128)} %slice_bitcast_fusion) | data formatting | bytes 1572864
  126.3 225.5 %all-reduce.2.cloned.1.call-done = f32[9,48,48]{1,2,0:T(8,128)} async-done(((f32[9,48,48]{1,2,0:T(8,128)}), f32[9,48,48]{1,2,0:T(8,128)}) %all-reduce.2.cloned.1.call-update) | async-done | bytes 82960 | tf_op jit(solution)/shard_map/psum | solution.py:83
  351.8 1.0 broadcast_multiply_fusion
  352.7 0.8 copy.70
  (8 shorter events, 0.2 us)
Async XLA Ops:
  7.2 1.9 copy-start.1
  7.2 344.6 %all-reduce.2.cloned.1.call-start = ((), (), s32[]{:S(2)}) async-start(), calls=%async_computation | async-start | bytes 442368 | tf_op jit(solution)/shard_map/psum | solution.py:83
  11.1 11.7 %copy-start.3 = (f32[9,48,48]{2,1,0:T(8,128)S(1)}, f32[9,48,48]{2,1,0:T(8,128)}, u32[]{:S(2)}) copy-start(f32[9,48,48]{2,1,0:T(8,128)} %param.8) | copy-start | bytes 248836
  12.1 10.9 %collective-permute-start = (f32[96,1,128]{0,2,1:T(8,128)S(1)}, f32[96,1,128]{0,2,1:T(8,128)S(1)}, u32[]{:S(2)}, u32[]{:S(2)}) collective-permute-start(f32[96,1,128]{0,2,1:T(8,128)S(1)} %get-tuple-element.39), channel_id=1, source_target_pairs={{0,8},{8,16},{16,24},{24,32},{32,40},{40,48},{48,56},{56,64},{64,7... | collective-permute-start | bytes 147464 | tf_op jit(solution)/shard_map/ppermute | solution.py:17
  19.3 6.5 %collective-permute-start.1 = (f32[96,1,128]{0,2,1:T(8,128)S(1)}, f32[96,1,128]{0,2,1:T(8,128)S(1)}, u32[]{:S(2)}, u32[]{:S(2)}) collective-permute-start(f32[96,1,128]{0,2,1:T(8,128)S(1)} %get-tuple-element.40), channel_id=1, source_target_pairs={{8,0},{16,8},{24,16},{32,24},{40,32},{48,40},{56,48},{64,56},{72,6... | collective-permute-start | bytes 147464 | tf_op jit(solution)/shard_map/ppermute | solution.py:19
  26.9 12.9 %collective-permute-start.3 = (f32[96,34,1]{0,2,1:T(1,128)S(1)}, f32[96,34,1]{0,2,1:T(1,128)S(1)}, u32[]{:S(2)}, u32[]{:S(2)}) collective-permute-start(f32[96,34,1]{0,2,1:T(1,128)S(1)} %get-tuple-element.37), channel_id=1, source_target_pairs={{0,1},{1,2},{2,3},{3,4},{4,5},{5,6},{6,7},{8,9},{9,10},{10,11},{11... | collective-permute-start | bytes 39176 | tf_op jit(solution)/shard_map/ppermute | solution.py:17
  31.2 8.5 %collective-permute-start.4 = (f32[96,34,1]{0,2,1:T(1,128)S(1)}, f32[96,34,1]{0,2,1:T(1,128)S(1)}, u32[]{:S(2)}, u32[]{:S(2)}) collective-permute-start(f32[96,34,1]{0,2,1:T(1,128)S(1)} %get-tuple-element.38), channel_id=1, source_target_pairs={{1,0},{2,1},{3,2},{4,3},{5,4},{6,5},{7,6},{9,8},{10,9},{11,10},{12... | collective-permute-start | bytes 39176 | tf_op jit(solution)/shard_map/ppermute | solution.py:19
  32.5 8.7 %collective-permute-start.2 = (f32[96,34,2]{0,2,1:T(2,128)S(1)}, f32[96,34,2]{0,2,1:T(2,128)S(1)}, u32[]{:S(2)}, u32[]{:S(2)}) collective-permute-start(f32[96,34,2]{0,2,1:T(2,128)S(1)} %pad_maximum_fusion.27), channel_id=1, source_target_pairs={{0,256},{8,264},{16,272},{24,280},{32,288},{40,296},{48,304},{56,3... | collective-permute-start | bytes 78344 | tf_op jit(solution)/shard_map/ppermute | solution.py:29
  53.6 3.4 copy-start
  79.8 0.7 copy-start.2
  87.2 0.7 copy-start.4
Sparse Core Ops, SparseCore 0:
  80.7 271.0 all-reduce.1
where the time goes:
time: 364 us; the launch traced here: 361 us
  waiting for transfers between devices  230 us (63%)
  matrix products  60.7 us (17%)
  starting transfers between devices  23.5 us (6%)
  local copies, waits for them, and re-layouts  16.9 us (5%)
  other arithmetic  15.2 us (4%)
  between operations  14.9 us (4%)
    psum x1, waiting for transfers between devices, body(): summed = lax.psum(local_weight, ('lon', 'lat'))  225 us
    dot_general x9, matrix products, body(): jnp.einsum('ohw,chw->oc', cotangent, window, precision=lax.Precision.HIGH...  33 us
    conv_general_dilated x4, matrix products, conv_valid(): lax.conv_general_dilated(grid[None], kernel, (1, 1), 'VALID', precision=l...  27.7 us
    ppermute x2, starting transfers between devices, padded(): lax.ppermute(tail, axis, [(i, (i + 1) % count) for i in range(ends)])  11.5 us
    unnamed x15, local copies, waits for them, and re-layouts  11.2 us
  transfers between devices with their start and end apart: 6, of which 3 were waited for; matrix products, arithmetic and copies ran while one was open for 13% of the time, Pallas kernels for 0%

commit v1 on v0

v1 whole, which is shorter than its diff:
```python
import functools
import math

import jax
import jax.numpy as jnp
from jax import lax
from jax.experimental import pallas as pl
from jax.experimental.pallas import tpu as pltpu
from jax.sharding import PartitionSpec as P

CH = 48
COLS = 32
ROWS = 128
PART = 24
MESH = pl.DeviceIdType.MESH
F32 = jnp.float32
BF16 = jnp.bfloat16


def split(x):
    hi = x.astype(BF16)
    return hi, (x - hi.astype(F32)).astype(BF16)


def column(ref, j):
    return ref[pl.ds(j, CH, stride=COLS), :]


def dot_nn(a, b):
    return lax.dot_general(a, b, (((1,), (0,)), ((), ())), preferred_element_type=F32)


def dot_nt(a, b):
    return lax.dot_general(a, b, (((1,), (1,)), ((), ())), preferred_element_type=F32)


def remote(src, dst, send, recv, to):
    return pltpu.make_async_remote_copy(
        src_ref=src, dst_ref=dst, send_sem=send, recv_sem=recv,
        device_id=to, device_id_type=MESH,
    )


def kernel(scale, f_hbm, g_hbm, w_ref, resp_ref, gfield_ref, gw_ref,
           fv, gv, z, v, p, edge, halo, colout, colin, corner, cornerin,
           part, got, total, whole, in_sem, hs_sem, hr_sem, as_sem, ar_sem):
    lon = lax.axis_index("lon")
    lat = lax.axis_index("lat")
    n_lon = lax.axis_size("lon")
    n_lat = lax.axis_size("lat")
    y, zh, core = lon // 8, (lon // 2) % 4, lon % 2
    x, zl = lat // 2, lat % 2
    depth = zh * 2 + zl
    is_north = jnp.where(lat == 0, 1, 0)
    is_south = jnp.where(lat == n_lat - 1, 1, 0)
    opposite = (lon + n_lon // 2) % n_lon

    def place(x, y, depth, core):
        return (y * 8 + (depth // 2) * 2 + core, x * 2 + depth % 2)

    west = ((lon + n_lon - 1) % n_lon, lat)
    east = ((lon + 1) % n_lon, lat)
    north = (jnp.where(lat == 0, opposite, lon), jnp.where(lat == 0, 0, lat - 1))
    south = (jnp.where(lat == n_lat - 1, opposite, lon),
             jnp.where(lat == n_lat - 1, n_lat - 1, lat + 1))
    near = [(dx, dc) for dx in range(4) for dc in range(2) if (dx, dc) != (0, 0)]
    pool = [place((x + dx) % 4, y, depth, (core + dc) % 2) for dx, dc in near]
    pool_rank = [((x + dx) % 4) * 2 + (core + dc) % 2 for dx, dc in near]
    along_y = [place(x, (y + k) % 8, depth, core) for k in range(1, 8)]
    along_z = [place(x, y, (depth + k) % 8, core) for k in range(1, 8)]
    rank = x * 2 + core

    barrier = pltpu.get_barrier_semaphore()
    partners = [west, east, north, south] + pool + along_y + along_z
    for to in partners:
        pl.semaphore_signal(barrier, inc=1, device_id=to, device_id_type=MESH)
    load_f = pltpu.make_async_copy(f_hbm, fv, in_sem.at[0])
    load_g = pltpu.make_async_copy(g_hbm, gv, in_sem.at[1])
    load_f.start()
    load_g.start()
    v[0] = jnp.zeros((6 * CH, ROWS), BF16)
    v[COLS + 1] = jnp.zeros((6 * CH, ROWS), BF16)
    load_f.wait()
    load_g.wait()

    lane = lax.broadcasted_iota(jnp.int32, (CH, ROWS), 1)

    def pack(j, acc):
        acc = jnp.where(lane // 2 == j, pltpu.roll(column(fv, j), 2 * j + 1, 1), acc)
        return jnp.where(lane // 2 == j + 32, pltpu.roll(column(gv, j), (2 * j + 65) % 128, 1), acc)

    edge[...] = lax.fori_loop(0, COLS, pack, jnp.zeros((CH, ROWS), F32))
    for side, j in enumerate((0, COLS - 1)):
        colout[side, :CH] = column(fv, j)
        colout[side, CH:] = column(gv, j)

    pl.semaphore_wait(barrier, len(partners))

    from_north = jnp.where(lat == 0, 0, 1)
    from_south = jnp.where(lat == n_lat - 1, 1, 0)
    halo_out = [
        remote(edge, halo.at[from_north], hs_sem.at[0], hr_sem.at[from_north], north),
        remote(edge, halo.at[from_south], hs_sem.at[1], hr_sem.at[from_south], south),
        remote(colout.at[0], colin.at[1], hs_sem.at[2], hr_sem.at[3], west),
        remote(colout.at[1], colin.at[0], hs_sem.at[3], hr_sem.at[2], east),
    ]
    for copy in halo_out:
        copy.start()

    def put(ref, at, a, value):
        hi, lo = split(value)
        ref[at, a * CH:(a + 1) * CH] = hi
        ref[at, (3 + a) * CH:(4 + a) * CH] = lo

    def shifted_down(value):
        return jnp.where(lane == 0, 0.0, pltpu.roll(value, 1, 1))

    def shifted_up(value):
        return jnp.where(lane == ROWS - 1, 0.0, pltpu.roll(value, ROWS - 1, 1))

    def build_plain(value, at):
        put(z, at, 0, shifted_down(value))
        put(z, at, 1, value)
        put(z, at, 2, shifted_up(value))

    def first_build(j, carry):
        build_plain(column(fv, j), j + 1)
        put(v, j + 1, 1, column(gv, j))
        return carry

    lax.fori_loop(0, COLS, first_build, 0)

    def weight_step(lhs_hi, lhs_lo, rhs_hi, rhs_lo):
        return dot_nt(lhs_hi, rhs_hi) + dot_nt(lhs_lo, rhs_hi) + dot_nt(lhs_hi, rhs_lo)

    def local_weight(s, acc):
        sides = [[], [], [], []]
        for k in range(4):
            at = s * 4 + k + 1
            for low in range(2):
                r = (1 + 3 * low) * CH
                sides[low].append(jnp.concatenate(
                    [v[at + 1, r:r + CH], v[at, r:r + CH], v[at - 1, r:r + CH]], axis=0))
                sides[2 + low].append(z[at, 3 * CH * low:3 * CH * (low + 1)])
        return acc + weight_step(*[jnp.concatenate(s, axis=1) for s in sides])

    acc = lax.fori_loop(0, COLS // 4, local_weight, jnp.zeros((3 * CH, 3 * CH), F32))

    forward = jnp.concatenate(
        [jnp.concatenate([w_ref[3 * a + b] for a in range(3)], axis=1) for b in range(3)], axis=0)
    turned = jnp.concatenate(
        [jnp.concatenate([w_ref[3 * (2 - a) + 2 - b] for b in range(3)], axis=1) for a in range(3)], axis=0)
    turned = jnp.concatenate([turned, jnp.zeros((3 * CH, 256 - 3 * CH), F32)], axis=1)
    turned = jnp.concatenate([turned, jnp.zeros((256 - 3 * CH, 256), F32)], axis=0)
    adjoint = turned.T[:3 * CH, :3 * CH]
    fwd_hi, fwd_lo = split(forward)
    adj_hi, adj_lo = split(adjoint)

    remote(edge, halo.at[0], hs_sem.at[0], hr_sem.at[0], north).wait_recv()
    remote(edge, halo.at[1], hs_sem.at[1], hr_sem.at[1], south).wait_recv()
    beyond = jnp.where(
        lane % 2 == 0,
        pltpu.roll(halo[1], 1 + is_south, 1),
        pltpu.roll(halo[0], 3 - is_north, 1),
    )
    corner[...] = beyond
    remote(colout.at[0], colin.at[1], hs_sem.at[2], hr_sem.at[3], west).wait_recv()
    remote(colout.at[1], colin.at[0], hs_sem.at[3], hr_sem.at[2], east).wait_recv()

    build_plain(colin[0, :CH], 0)
    build_plain(colin[1, :CH], COLS + 1)
    blank = jnp.zeros((CH, ROWS), BF16)
    outer = []
    for low in range(2):
        r = (1 + 3 * low) * CH
        outer.append(jnp.concatenate([
            jnp.concatenate([v[1, r:r + CH], blank], axis=1),
            jnp.concatenate([blank, blank], axis=1),
            jnp.concatenate([blank, v[COLS, r:r + CH]], axis=1)], axis=0))
    for low in range(2):
        r = 3 * CH * low
        outer.append(jnp.concatenate([z[0, r:r + 3 * CH], z[COLS + 1, r:r + 3 * CH]], axis=1))
    acc = acc + weight_step(*outer)

    def packed(value, left):
        hi = value.astype(BF16).astype(F32)
        lo = (value - hi).astype(BF16).astype(F32)
        first, second = (lo, hi) if left else (hi, lo)
        return jnp.concatenate([hi + pltpu.roll(first, 64, 1), second], axis=1).astype(BF16)

    own = edge[...]
    inside = lane < 64
    left_rows = []
    for b in (-1, 0, 1):
        value = pltpu.roll(own, (64 + 2 * b) % 128, 1)
        if b == 1:
            value = jnp.where(lane < 2, pltpu.roll(colin[0, CH:], 1, 1), value)
        if b == -1:
            value = jnp.where(lane >= 62, pltpu.roll(colin[1, CH:], 63, 1), value)
        left_rows.append(packed(jnp.where(inside, value, 0.0), True))
    across = pltpu.roll(beyond, 126, 1)
    right_rows = [
        packed(jnp.where(inside & (lane % 2 == 1), across, 0.0), False),
        jnp.zeros((CH, 256), BF16),
        packed(jnp.where(inside & (lane % 2 == 0), across, 0.0), False),
    ]
    acc = acc + dot_nt(jnp.concatenate(left_rows, axis=0), jnp.concatenate(right_rows, axis=0))

    part[:3 * CH] = acc[:, :128]
    tail = jnp.concatenate([acc[:, 128:], jnp.zeros((3 * CH, 112), F32)], axis=1)
    part[3 * CH:] = (tail[:CH] + pltpu.roll(tail[CH:2 * CH], 16, 1)
                     + pltpu.roll(tail[2 * CH:], 32, 1))

    def reduce_scatter(k):
        return remote(part.at[pl.ds(pl.multiple_of(pool_rank[k] * PART, 8), PART)],
                      got.at[0, k], as_sem.at[0, k], ar_sem.at[0, k], pool[k])

    def exchange(phase, k, to, spot):
        return remote(total.at[phase - 1], got.at[phase, spot], as_sem.at[phase, k], ar_sem.at[phase, k], to)

    def share(phase):
        seat = seats[phase]
        got[phase, seat] = total[phase - 1]
        for k in range(7):
            exchange(phase, k, (along_y, along_z)[phase - 1][k], seat).start()

    def gather(k):
        return remote(total.at[2], whole.at[here], as_sem.at[3, k], ar_sem.at[3, k], pool[k])

    def arrive(phase):
        for k in range(7):
            if phase == 0:
                reduce_scatter(k).wait_recv()
            else:
                to = (along_y, along_z)[phase - 1][k]
                exchange(phase, k, to, (seats[phase] + 7 - k) % 8).wait_recv()
        value = part[here] if phase == 0 else got[phase, 7]
        for k in range(7):
            value = value + got[phase, k]
        total[phase] = value

    here = pl.ds(pl.multiple_of(rank * PART, 8), PART)
    seats = [None, y, depth]
    corners_out = [
        remote(corner, cornerin.at[1], hs_sem.at[4], hr_sem.at[5], west),
        remote(corner, cornerin.at[0], hs_sem.at[5], hr_sem.at[4], east),
    ]
    for k in range(7):
        reduce_scatter(k).start()
    for copy in corners_out:
        copy.start()

    first = jnp.where(lane == 0, 1.0, 0.0)
    last = jnp.where(lane == ROWS - 1, 1.0, 0.0)
    north_f = is_north.astype(F32)
    south_f = is_south.astype(F32)

    def build_whole(ref, value, at, ring, down, up):
        rim = pltpu.roll(ring, (127 - 2 * at) % 128, 1)
        put(ref, at, 0, shifted_down(value) + rim * down)
        put(ref, at, 1, value)
        put(ref, at, 2, shifted_up(value) + rim * up)

    adj_down = first * (1.0 - north_f) + last * south_f
    adj_up = last * (1.0 - south_f) + first * north_f

    def product(ref, hi, lo, left, right):
        rhs = jnp.concatenate([ref[left], ref[right]], axis=1)
        rhs_hi, rhs_lo = rhs[:3 * CH], rhs[3 * CH:]
        out = dot_nn(hi, rhs_hi) + dot_nn(lo, rhs_hi) + dot_nn(hi, rhs_lo)
        p[left] = out[:, :ROWS]
        p[right] = out[:, ROWS:]

    def inner_build(ref, src, ring, down, up):
        def step(j, carry):
            build_whole(ref, column(src, j), j + 1, ring, down, up)
            return carry
        lax.fori_loop(0, COLS, step, 0)

    def inner_products(ref, hi, lo):
        def step(s, carry):
            product(ref, hi, lo, 2 * s + 1, 2 * s + 2)
            return carry
        lax.fori_loop(0, COLS // 2, step, 0)

    def finish(out_ref):
        def step(j, carry):
            out_ref[pl.ds(j, CH, stride=COLS), :] = (
                p[j, :CH] + p[j + 1, CH:2 * CH] + p[j + 2, 2 * CH:])
            return carry
        lax.fori_loop(0, COLS, step, 0)

    ring_g = pltpu.roll(beyond, 64, 1)
    inner_build(z, fv, beyond, first, last)
    inner_products(z, fwd_hi, fwd_lo)

    arrive(0)
    share(1)

    remote(corner, cornerin.at[1], hs_sem.at[4], hr_sem.at[5], west).wait_recv()
    remote(corner, cornerin.at[0], hs_sem.at[5], hr_sem.at[4], east).wait_recv()
    from_west, from_east = cornerin[0], cornerin[1]
    ends_f = jnp.where(lane < 2, pltpu.roll(from_west, 64, 1), pltpu.roll(from_east, 64, 1))
    ends_g = jnp.where(lane < 2, from_west, from_east)
    for at, side in ((0, 0), (COLS + 1, 1)):
        build_whole(z, colin[side, :CH], at, ends_f, first, last)
        build_whole(v, colin[side, CH:], at, ends_g, adj_down, adj_up)
    product(z, fwd_hi, fwd_lo, 0, COLS + 1)
    finish(resp_ref)
    inner_build(v, gv, ring_g, adj_down, adj_up)

    arrive(1)
    share(2)
    inner_products(v, adj_hi, adj_lo)
    product(v, adj_hi, adj_lo, 0, COLS + 1)
    finish(gfield_ref)

    arrive(2)
    for k in range(7):
        gather(k).start()
    whole[here] = total[2]
    for k in range(7):
        peer = pl.ds(pl.multiple_of((((x + 4 - near[k][0]) % 4) * 2 + (core + near[k][1]) % 2) * PART, 8), PART)
        remote(total.at[2], whole.at[peer], as_sem.at[3, k], ar_sem.at[3, k], pool[k]).wait_recv()
    rest = whole[3 * CH:]
    for b in range(3):
        rows = whole[b * CH:(b + 1) * CH] * scale
        extra = pltpu.roll(rest, (32 - 16 * b) % 128, 1) * scale
        gw_ref[b] = rows[:, :CH]
        gw_ref[3 + b] = pltpu.roll(rows, 80, 1)[:, :CH]
        gw_ref[6 + b] = jnp.where(lane < 32, pltpu.roll(rows, 32, 1), extra)[:, :CH]

    for copy in halo_out + corners_out:
        copy.wait_send()
    for k in range(7):
        reduce_scatter(k).wait_send()
        exchange(1, k, along_y[k], y).wait_send()
        exchange(2, k, along_z[k], depth).wait_send()
        gather(k).wait_send()


def body(state_field, weight_bank, cotangent):
    cells = CH * COLS
    total_cells = ROWS * lax.axis_size("lat") * COLS * lax.axis_size("lon")
    whole = pl.BlockSpec(memory_space=pltpu.VMEM)
    far = pl.BlockSpec(memory_space=pl.ANY)
    response, grad_field, grad_weight = pl.pallas_call(
        functools.partial(kernel, 1.0 / math.sqrt(total_cells)),
        out_shape=[
            jax.ShapeDtypeStruct((cells, ROWS), F32),
            jax.ShapeDtypeStruct((cells, ROWS), F32),
            jax.ShapeDtypeStruct((9, CH, CH), F32),
        ],
        in_specs=[far, far, whole],
        out_specs=[whole, whole, whole],
        scratch_shapes=[
            pltpu.VMEM((cells, ROWS), F32),
            pltpu.VMEM((cells, ROWS), F32),
            pltpu.VMEM((COLS + 2, 6 * CH, ROWS), BF16),
            pltpu.VMEM((COLS + 2, 6 * CH, ROWS), BF16),
            pltpu.VMEM((COLS + 2, 3 * CH, ROWS), F32),
            pltpu.VMEM((CH, ROWS), F32),
            pltpu.VMEM((2, CH, ROWS), F32),
            pltpu.VMEM((2, 2 * CH, ROWS), F32),
            pltpu.VMEM((2, 2 * CH, ROWS), F32),
            pltpu.VMEM((CH, ROWS), F32),
            pltpu.VMEM((2, CH, ROWS), F32),
            pltpu.VMEM((8 * PART, ROWS), F32),
            pltpu.VMEM((3, 8, PART, ROWS), F32),
            pltpu.VMEM((3, PART, ROWS), F32),
            pltpu.VMEM((8 * PART, ROWS), F32),
            pltpu.SemaphoreType.DMA((2,)),
            pltpu.SemaphoreType.DMA((6,)),
            pltpu.SemaphoreType.DMA((6,)),
            pltpu.SemaphoreType.DMA((4, 7)),
            pltpu.SemaphoreType.DMA((4, 7)),
        ],
        compiler_params=pltpu.CompilerParams(
            collective_id=0, has_side_effects=True, vmem_limit_bytes=40 << 20
        ),
        cost_estimate=pl.CostEstimate(
            flops=3 * 3 * 9 * CH * CH * COLS * ROWS * 2, bytes_accessed=16 * cells * ROWS, transcendentals=0
        ),
    )(state_field.reshape(cells, ROWS), cotangent.reshape(cells, ROWS), weight_bank)
    shape = (CH, COLS, ROWS)
    return response.reshape(shape), grad_field.reshape(shape), grad_weight


def solution(mesh):
    in_specs = (P(None, "lon", "lat"), P(), P(None, "lon", "lat"))
    out_specs = (P(None, "lon", "lat"), P(None, "lon", "lat"), P())
    return jax.shard_map(body, mesh=mesh, in_specs=in_specs, out_specs=out_specs, check_vma=False)
```

time: 364 us -> 53 us (0.15)
  waiting for transfers between devices: 230 us -> 0 us
  matrix products: 60.7 us -> 0 us
  Pallas kernels: 0 us -> 46.5 us
  starting transfers between devices: 23.5 us -> 0 us
  other arithmetic: 15.2 us -> 0 us
  between operations: 14.9 us -> 0.65 us
  local copies, waits for them, and re-layouts: 16.9 us -> 5.64 us
    psum x1 -> x0, waiting for transfers between devices: 225 us -> none  [body(): summed = lax.psum(local_weight, ('lon', 'lat'))]
    pallas_call x0 -> x1, Pallas kernels: none -> 46.5 us  [body(): pl.pallas_call(functools.partial(kernel, 1.0 / math.sqrt(total_cells)), o...]
    dot_general x9 -> x0, matrix products: 33 us -> none  [body(): jnp.einsum('ohw,chw->oc', cotangent, window, precision=lax.Precision.HIGH...]
    conv_general_dilated x4 -> x0, matrix products: 27.7 us -> none  [conv_valid(): lax.conv_general_dilated(grid[None], kernel, (1, 1), 'VALID', precision=l...]
    ppermute x5 -> x0, starting transfers between devices: 23.4 us -> none  [the longest x2 11.5 us: padded(): lax.ppermute(tail, axis, [(i, (i + 1) % count) for i in range(ends)])]
    broadcast_in_dim x1 -> x0, other arithmetic: 6.51 us -> none  [conv_valid(): grid[None]]
    unnamed x15 -> x9, local copies, waits for them, and re-layouts: 11.2 us -> 5.64 us
    concatenate x2 -> x0, other arithmetic: 5.36 us -> none  [the longest x1 5.32 us: extend_grid(): return jnp.concatenate([first_row, banded[:, :, 1:-1], final_row], axis=2)]
  transfers between devices with their start and end apart: 6 -> 0, of which waited for: 3 -> 0; matrix products, arithmetic and copies ran while one was open for 13% -> 0% of each run, Pallas kernels for 0% -> 0%
where the time goes in v1:
time: 53 us; the launch traced here: 52.8 us
  Pallas kernels  46.5 us (88%)
  local copies, waits for them, and re-layouts  5.64 us (11%)
  between operations  0.65 us (1%)
    pallas_call x1, Pallas kernels, body(): pl.pallas_call(functools.partial(kernel, 1.0 / math.sqrt(total_cells)), o...  46.5 us
    unnamed x9, local copies, waits for them, and re-layouts  5.64 us

profile of v1, /device:TPU:1, one launch (start us, length us, event | category | flops | bytes accessed | tf_op | source)
XLA Modules:
  0.0 52.8 jit_solution(12749390405828320957)
XLA Ops:
  0.6 0.0 copy-start
  0.6 1.1 %copy-done = f32[48,32,128]{2,1,0:T(8,128)S(1)} copy-done((f32[48,32,128]{2,1,0:T(8,128)S(1)}, f32[48,32,128]{2,1,0:T(8,128)}, u32[]{:S(2)}) %copy-start) | copy-done | bytes 786456
  1.8 0.0 copy-start.1
  1.8 1.1 %copy-done.1 = f32[48,32,128]{2,1,0:T(8,128)S(1)} copy-done((f32[48,32,128]{2,1,0:T(8,128)S(1)}, f32[48,32,128]{2,1,0:T(8,128)}, u32[]{:S(2)}) %copy-start.1) | copy-done | bytes 786456
  2.9 0.0 copy-start.2
  2.9 0.9 %copy-done.2 = f32[9,48,48]{2,1,0:T(8,128)S(1)} copy-done((f32[9,48,48]{2,1,0:T(8,128)S(1)}, f32[9,48,48]{2,1,0:T(8,128)}, u32[]{:S(2)}) %copy-start.2) | copy-done | bytes 82968
  3.8 46.5 %shard_map.58 = (f32[1536,128]{1,0:T(8,128)S(1)}, f32[1536,128]{1,0:T(8,128)S(1)}, f32[9,48,48]{2,1,0:T(8,128)S(1)}) custom-call(f32[1536,128]{1,0:T(8,128)S(1)} %bitcast.6, f32[1536,128]{1,0:T(8,128)S(1)} %bitcast.7, f32[9,48,48]{2,1,0:T(8,128)S(1)} %copy-done.2), custom_call_target="tpu_custom_call" | custom-call | flops 1528823808 | bytes 3145728 | tf_op jit(solution)/shard_map/pallas_call | solution.py:347
  50.3 0.9 %copy.9 = f32[48,32,128]{2,1,0:T(8,128)} copy(f32[48,32,128]{2,1,0:T(8,128)S(1)} %bitcast.5) | data formatting | bytes 1572864
  51.2 0.9 %copy.10 = f32[48,32,128]{2,1,0:T(8,128)} copy(f32[48,32,128]{2,1,0:T(8,128)S(1)} %bitcast.4) | data formatting | bytes 1572864
  52.1 0.7 %copy.11 = f32[9,48,48]{2,1,0:T(8,128)} copy(f32[9,48,48]{2,1,0:T(8,128)S(1)} %get-tuple-element.14) | data formatting | bytes 165888
Async XLA Ops:
  0.6 1.1 %copy-start = (f32[48,32,128]{2,1,0:T(8,128)S(1)}, f32[48,32,128]{2,1,0:T(8,128)}, u32[]{:S(2)}) copy-start(f32[48,32,128]{2,1,0:T(8,128)} %param.3) | copy-start | bytes 2359300
  1.8 1.1 %copy-start.1 = (f32[48,32,128]{2,1,0:T(8,128)S(1)}, f32[48,32,128]{2,1,0:T(8,128)}, u32[]{:S(2)}) copy-start(f32[48,32,128]{2,1,0:T(8,128)} %param.5) | copy-start | bytes 2359300
  2.9 0.9 %copy-start.2 = (f32[9,48,48]{2,1,0:T(8,128)S(1)}, f32[9,48,48]{2,1,0:T(8,128)}, u32[]{:S(2)}) copy-start(f32[9,48,48]{2,1,0:T(8,128)} %w_ref.1) | copy-start | bytes 248836

commit v2 on v1

--- a/solution.py
+++ b/solution.py
@@ -41,8 +41,8 @@
     )
 
 
-def kernel(scale, f_hbm, g_hbm, w_ref, resp_ref, gfield_ref, gw_ref,
-           fv, gv, z, v, p, edge, halo, colout, colin, corner, cornerin,
+def kernel(f_hbm, g_hbm, w_hbm, resp, gfield, final,
+           fv, gv, w_ref, z, v, p, q, edge, halo, colout, colin, corner, cornerin,
            part, got, total, whole, in_sem, hs_sem, hr_sem, as_sem, ar_sem):
     lon = lax.axis_index("lon")
     lat = lax.axis_index("lat")
@@ -76,8 +76,10 @@
         pl.semaphore_signal(barrier, inc=1, device_id=to, device_id_type=MESH)
     load_f = pltpu.make_async_copy(f_hbm, fv, in_sem.at[0])
     load_g = pltpu.make_async_copy(g_hbm, gv, in_sem.at[1])
+    load_w = pltpu.make_async_copy(w_hbm, w_ref, in_sem.at[2])
     load_f.start()
     load_g.start()
+    load_w.start()
     v[0] = jnp.zeros((6 * CH, ROWS), BF16)
     v[COLS + 1] = jnp.zeros((6 * CH, ROWS), BF16)
     load_f.wait()
@@ -89,10 +91,26 @@
         acc = jnp.where(lane // 2 == j, pltpu.roll(column(fv, j), 2 * j + 1, 1), acc)
         return jnp.where(lane // 2 == j + 32, pltpu.roll(column(gv, j), (2 * j + 65) % 128, 1), acc)
 
-    edge[...] = lax.fori_loop(0, COLS, pack, jnp.zeros((CH, ROWS), F32))
+    edge[...] = lax.fori_loop(0, COLS, pack, jnp.zeros((CH, ROWS), F32), unroll=8)
     for side, j in enumerate((0, COLS - 1)):
         colout[side, :CH] = column(fv, j)
         colout[side, CH:] = column(gv, j)
+
+    def put(ref, at, a, value):
+        hi, lo = split(value)
+        ref[at, a * CH:(a + 1) * CH] = hi
+        ref[at, (3 + a) * CH:(4 + a) * CH] = lo
+
+    def build(ref, at, value):
+        put(ref, at, 0, jnp.where(lane == 0, 0.0, pltpu.roll(value, 1, 1)))
+        put(ref, at, 1, value)
+        put(ref, at, 2, jnp.where(lane == ROWS - 1, 0.0, pltpu.roll(value, ROWS - 1, 1)))
+
+    def build_all(ref, src):
+        def step(j, carry):
+            build(ref, j + 1, column(src, j))
+            return carry
+        lax.fori_loop(0, COLS, step, 0, unroll=8)
 
     pl.semaphore_wait(barrier, len(partners))
 
@@ -107,36 +125,16 @@
     for copy in halo_out:
         copy.start()
 
-    def put(ref, at, a, value):
-        hi, lo = split(value)
-        ref[at, a * CH:(a + 1) * CH] = hi
-        ref[at, (3 + a) * CH:(4 + a) * CH] = lo
-
-    def shifted_down(value):
-        return jnp.where(lane == 0, 0.0, pltpu.roll(value, 1, 1))
-
-    def shifted_up(value):
-        return jnp.where(lane == ROWS - 1, 0.0, pltpu.roll(value, ROWS - 1, 1))
-
-    def build_plain(value, at):
-        put(z, at, 0, shifted_down(value))
-        put(z, at, 1, value)
-        put(z, at, 2, shifted_up(value))
-
-    def first_build(j, carry):
-        build_plain(column(fv, j), j + 1)
-        put(v, j + 1, 1, column(gv, j))
-        return carry
-
-    lax.fori_loop(0, COLS, first_build, 0)
+    build_all(z, fv)
+    build_all(v, gv)
 
     def weight_step(lhs_hi, lhs_lo, rhs_hi, rhs_lo):
         return dot_nt(lhs_hi, rhs_hi) + dot_nt(lhs_lo, rhs_hi) + dot_nt(lhs_hi, rhs_lo)
 
     def local_weight(s, acc):
         sides = [[], [], [], []]
-        for k in range(4):
-            at = s * 4 + k + 1
+        for k in range(16):
+            at = s * 16 + k + 1
             for low in range(2):
                 r = (1 + 3 * low) * CH
                 sides[low].append(jnp.concatenate(
@@ -144,8 +142,9 @@
                 sides[2 + low].append(z[at, 3 * CH * low:3 * CH * (low + 1)])
         return acc + weight_step(*[jnp.concatenate(s, axis=1) for s in sides])
 
-    acc = lax.fori_loop(0, COLS // 4, local_weight, jnp.zeros((3 * CH, 3 * CH), F32))
-
+    acc = lax.fori_loop(0, COLS // 16, local_weight, jnp.zeros((3 * CH, 3 * CH), F32))
+
+    load_w.wait()
     forward = jnp.concatenate(
         [jnp.concatenate([w_ref[3 * a + b] for a in range(3)], axis=1) for b in range(3)], axis=0)
     turned = jnp.concatenate(
@@ -156,19 +155,25 @@
     fwd_hi, fwd_lo = split(forward)
     adj_hi, adj_lo = split(adjoint)
 
-    remote(edge, halo.at[0], hs_sem.at[0], hr_sem.at[0], north).wait_recv()
-    remote(edge, halo.at[1], hs_sem.at[1], hr_sem.at[1], south).wait_recv()
-    beyond = jnp.where(
-        lane % 2 == 0,
-        pltpu.roll(halo[1], 1 + is_south, 1),
-        pltpu.roll(halo[0], 3 - is_north, 1),
-    )
-    corner[...] = beyond
+    def product(out, ref, hi, lo, left, right):
+        rhs = jnp.concatenate([ref[left], ref[right]], axis=1)
+        rhs_hi, rhs_lo = rhs[:3 * CH], rhs[3 * CH:]
+        value = dot_nn(hi, rhs_hi) + dot_nn(lo, rhs_hi) + dot_nn(hi, rhs_lo)
+        out[left] = value[:, :ROWS]
+        out[right] = value[:, ROWS:]
+
+    def products(out, ref, hi, lo):
+        def step(s, carry):
+            product(out, ref, hi, lo, 2 * s + 1, 2 * s + 2)
+            return carry
+        lax.fori_loop(0, COLS // 2, step, 0, unroll=4)
+
+
     remote(colout.at[0], colin.at[1], hs_sem.at[2], hr_sem.at[3], west).wait_recv()
     remote(colout.at[1], colin.at[0], hs_sem.at[3], hr_sem.at[2], east).wait_recv()
 
-    build_plain(colin[0, :CH], 0)
-    build_plain(colin[1, :CH], COLS + 1)
+    build(z, 0, colin[0, :CH])
+    build(z, COLS + 1, colin[1, :CH])
     blank = jnp.zeros((CH, ROWS), BF16)
     outer = []
     for low in range(2):
@@ -198,6 +203,14 @@
         if b == -1:
             value = jnp.where(lane >= 62, pltpu.roll(colin[1, CH:], 63, 1), value)
         left_rows.append(packed(jnp.where(inside, value, 0.0), True))
+    remote(edge, halo.at[0], hs_sem.at[0], hr_sem.at[0], north).wait_recv()
+    remote(edge, halo.at[1], hs_sem.at[1], hr_sem.at[1], south).wait_recv()
+    beyond = jnp.where(
+        lane % 2 == 0,
+        pltpu.roll(halo[1], 1 + is_south, 1),
+        pltpu.roll(halo[0], 3 - is_north, 1),
+    )
+    corner[...] = beyond
     across = pltpu.roll(beyond, 126, 1)
     right_rows = [
         packed(jnp.where(inside & (lane % 2 == 1), across, 0.0), False),
@@ -250,49 +263,12 @@
     for copy in corners_out:
         copy.start()
 
-    first = jnp.where(lane == 0, 1.0, 0.0)
-    last = jnp.where(lane == ROWS - 1, 1.0, 0.0)
-    north_f = is_north.astype(F32)
-    south_f = is_south.astype(F32)
-
-    def build_whole(ref, value, at, ring, down, up):
-        rim = pltpu.roll(ring, (127 - 2 * at) % 128, 1)
-        put(ref, at, 0, shifted_down(value) + rim * down)
-        put(ref, at, 1, value)
-        put(ref, at, 2, shifted_up(value) + rim * up)
-
-    adj_down = first * (1.0 - north_f) + last * south_f
-    adj_up = last * (1.0 - south_f) + first * north_f
-
-    def product(ref, hi, lo, left, right):
-        rhs = jnp.concatenate([ref[left], ref[right]], axis=1)
-        rhs_hi, rhs_lo = rhs[:3 * CH], rhs[3 * CH:]
-        out = dot_nn(hi, rhs_hi) + dot_nn(lo, rhs_hi) + dot_nn(hi, rhs_lo)
-        p[left] = out[:, :ROWS]
-        p[right] = out[:, ROWS:]
-
-    def inner_build(ref, src, ring, down, up):
-        def step(j, carry):
-            build_whole(ref, column(src, j), j + 1, ring, down, up)
-            return carry
-        lax.fori_loop(0, COLS, step, 0)
-
-    def inner_products(ref, hi, lo):
-        def step(s, carry):
-            product(ref, hi, lo, 2 * s + 1, 2 * s + 2)
-            return carry
-        lax.fori_loop(0, COLS // 2, step, 0)
-
-    def finish(out_ref):
-        def step(j, carry):
-            out_ref[pl.ds(j, CH, stride=COLS), :] = (
-                p[j, :CH] + p[j + 1, CH:2 * CH] + p[j + 2, 2 * CH:])
-            return carry
-        lax.fori_loop(0, COLS, step, 0)
-
-    ring_g = pltpu.roll(beyond, 64, 1)
-    inner_build(z, fv, beyond, first, last)
-    inner_products(z, fwd_hi, fwd_lo)
+    products(p, z, fwd_hi, fwd_lo)
+    products(q, v, adj_hi, adj_lo)
+    build(v, 0, colin[0, CH:])
+    build(v, COLS + 1, colin[1, CH:])
+    product(p, z, fwd_hi, fwd_lo, 0, COLS + 1)
+    product(q, v, adj_hi, adj_lo, 0, COLS + 1)
 
     arrive(0)
     share(1)
@@ -300,20 +276,36 @@
     remote(corner, cornerin.at[1], hs_sem.at[4], hr_sem.at[5], west).wait_recv()
     remote(corner, cornerin.at[0], hs_sem.at[5], hr_sem.at[4], east).wait_recv()
     from_west, from_east = cornerin[0], cornerin[1]
-    ends_f = jnp.where(lane < 2, pltpu.roll(from_west, 64, 1), pltpu.roll(from_east, 64, 1))
-    ends_g = jnp.where(lane < 2, from_west, from_east)
-    for at, side in ((0, 0), (COLS + 1, 1)):
-        build_whole(z, colin[side, :CH], at, ends_f, first, last)
-        build_whole(v, colin[side, CH:], at, ends_g, adj_down, adj_up)
-    product(z, fwd_hi, fwd_lo, 0, COLS + 1)
-    finish(resp_ref)
-    inner_build(v, gv, ring_g, adj_down, adj_up)
+
+    def finish(out, src, kernel_n, kernel_s, ring):
+        weight_hi, weight_lo = split(jnp.concatenate([kernel_n, kernel_s], axis=1))
+        odd = lane % 2 == 1
+        ring_hi, ring_lo = split(jnp.concatenate(
+            [jnp.where(odd, ring, 0.0), jnp.where(odd, 0.0, ring)], axis=0))
+        terms = dot_nn(weight_hi, ring_hi) + dot_nn(weight_lo, ring_hi) + dot_nn(weight_hi, ring_lo)
+        terms = (pltpu.roll(terms[:CH], 2, 1) + terms[CH:2 * CH]
+                 + pltpu.roll(terms[2 * CH:], ROWS - 2, 1))
+        rim = (lane == 0) | (lane == ROWS - 1)
+
+        def step(j, carry):
+            value = src[j, :CH] + src[j + 1, CH:2 * CH] + src[j + 2, 2 * CH:]
+            value = value + jnp.where(rim, pltpu.roll(terms, 125 - 2 * j, 1), 0.0)
+            out[pl.ds(j, CH, stride=COLS), :] = value
+            return carry
+
+        lax.fori_loop(0, COLS, step, 0, unroll=8)
+
+    middle = (lane >= 2) & (lane < 66)
+    ring_f = jnp.where(middle, beyond, jnp.where(
+        lane < 2, pltpu.roll(from_west, 64, 1), pltpu.roll(from_east, 64, 1)))
+    finish(resp, p, forward[:, :CH], forward[:, 2 * CH:], ring_f)
 
     arrive(1)
     share(2)
-    inner_products(v, adj_hi, adj_lo)
-    product(v, adj_hi, adj_lo, 0, COLS + 1)
-    finish(gfield_ref)
+    low_side, high_side = adjoint[:, :CH], adjoint[:, 2 * CH:]
+    ring_g = jnp.where(middle, pltpu.roll(beyond, 64, 1), jnp.where(lane < 2, from_west, from_east))
+    finish(gfield, q, jnp.where(lat == 0, high_side, low_side),
+           jnp.where(lat == n_lat - 1, low_side, high_side), ring_g)
 
     arrive(2)
     for k in range(7):
@@ -322,14 +314,7 @@
     for k in range(7):
         peer = pl.ds(pl.multiple_of((((x + 4 - near[k][0]) % 4) * 2 + (core + near[k][1]) % 2) * PART, 8), PART)
         remote(total.at[2], whole.at[peer], as_sem.at[3, k], ar_sem.at[3, k], pool[k]).wait_recv()
-    rest = whole[3 * CH:]
-    for b in range(3):
-        rows = whole[b * CH:(b + 1) * CH] * scale
-        extra = pltpu.roll(rest, (32 - 16 * b) % 128, 1) * scale
-        gw_ref[b] = rows[:, :CH]
-        gw_ref[3 + b] = pltpu.roll(rows, 80, 1)[:, :CH]
-        gw_ref[6 + b] = jnp.where(lane < 32, pltpu.roll(rows, 32, 1), extra)[:, :CH]
-
+    final[...] = whole[...]
     for copy in halo_out + corners_out:
         copy.wait_send()
     for k in range(7):
@@ -339,25 +324,47 @@
         gather(k).wait_send()
 
 
+def hand_over(scale, resp, gfield, final, resp_hbm, gfield_hbm, gw_hbm, gw, sem):
+    stores = [
+        pltpu.make_async_copy(resp, resp_hbm, sem.at[0]),
+        pltpu.make_async_copy(gfield, gfield_hbm, sem.at[1]),
+        pltpu.make_async_copy(gw, gw_hbm, sem.at[2]),
+    ]
+    stores[0].start()
+    stores[1].start()
+    lane = lax.broadcasted_iota(jnp.int32, (CH, ROWS), 1)
+    rest = final[3 * CH:]
+    for b in range(3):
+        rows = final[b * CH:(b + 1) * CH] * scale
+        extra = pltpu.roll(rest, (32 - 16 * b) % 128, 1) * scale
+        gw[b] = rows[:, :CH]
+        gw[3 + b] = pltpu.roll(rows, 80, 1)[:, :CH]
+        gw[6 + b] = jnp.where(lane < 32, pltpu.roll(rows, 32, 1), extra)[:, :CH]
+    stores[2].start()
+    for copy in stores:
+        copy.wait()
+
+
 def body(state_field, weight_bank, cotangent):
     cells = CH * COLS
     total_cells = ROWS * lax.axis_size("lat") * COLS * lax.axis_size("lon")
-    whole = pl.BlockSpec(memory_space=pltpu.VMEM)
-    far = pl.BlockSpec(memory_space=pl.ANY)
-    response, grad_field, grad_weight = pl.pallas_call(
-        functools.partial(kernel, 1.0 / math.sqrt(total_cells)),
-        out_shape=[
-            jax.ShapeDtypeStruct((cells, ROWS), F32),
-            jax.ShapeDtypeStruct((cells, ROWS), F32),
-            jax.ShapeDtypeStruct((9, CH, CH), F32),
-        ],
-        in_specs=[far, far, whole],
-        out_specs=[whole, whole, whole],
+    near = pl.BlockSpec(memory_space=pltpu.VMEM)
+    far = pl.BlockSpec(memory_space=pltpu.HBM)
+    field = jax.ShapeDtypeStruct((cells, ROWS), F32)
+    held = lambda *dims: pltpu.VMEM(dims, F32)
+    pinned = lambda value: pltpu.with_memory_space_constraint(value, pltpu.HBM)
+    parts = pl.pallas_call(
+        kernel,
+        out_shape=[held(cells, ROWS), held(cells, ROWS), held(8 * PART, ROWS)],
+        in_specs=[far, far, far],
+        out_specs=[near, near, near],
         scratch_shapes=[
             pltpu.VMEM((cells, ROWS), F32),
             pltpu.VMEM((cells, ROWS), F32),
+            pltpu.VMEM((9, CH, CH), F32),
             pltpu.VMEM((COLS + 2, 6 * CH, ROWS), BF16),
             pltpu.VMEM((COLS + 2, 6 * CH, ROWS), BF16),
+            pltpu.VMEM((COLS + 2, 3 * CH, ROWS), F32),
             pltpu.VMEM((COLS + 2, 3 * CH, ROWS), F32),
             pltpu.VMEM((CH, ROWS), F32),
             pltpu.VMEM((2, CH, ROWS), F32),
@@ -369,7 +376,7 @@
             pltpu.VMEM((3, 8, PART, ROWS), F32),
             pltpu.VMEM((3, PART, ROWS), F32),
             pltpu.VMEM((8 * PART, ROWS), F32),
-            pltpu.SemaphoreType.DMA((2,)),
+            pltpu.SemaphoreType.DMA((3,)),
             pltpu.SemaphoreType.DMA((6,)),
             pltpu.SemaphoreType.DMA((6,)),
             pltpu.SemaphoreType.DMA((4, 7)),
@@ -381,7 +388,14 @@
         cost_estimate=pl.CostEstimate(
             flops=3 * 3 * 9 * CH * CH * COLS * ROWS * 2, bytes_accessed=16 * cells * ROWS, transcendentals=0
         ),
-    )(state_field.reshape(cells, ROWS), cotangent.reshape(cells, ROWS), weight_bank)
+    )(pinned(state_field.reshape(cells, ROWS)), pinned(cotangent.reshape(cells, ROWS)), pinned(weight_bank))
+    response, grad_field, grad_weight = pl.pallas_call(
+        functools.partial(hand_over, 1.0 / math.sqrt(total_cells)),
+        out_shape=[field, field, jax.ShapeDtypeStruct((9, CH, CH), F32)],
+        in_specs=[near, near, near],
+        out_specs=[far, far, far],
+        scratch_shapes=[pltpu.VMEM((9, CH, CH), F32), pltpu.SemaphoreType.DMA((3,))],
+    )(*[pltpu.with_memory_space_constraint(value, pltpu.VMEM) for value in parts])
     shape = (CH, COLS, ROWS)
     return response.reshape(shape), grad_field.reshape(shape), grad_weight
 

time: 53 us -> 43.1 us (0.81)
  local copies, waits for them, and re-layouts: 5.64 us -> 0 us
  Pallas kernels: 46.5 us -> 42.4 us
    unnamed x9 -> x0, local copies, waits for them, and re-layouts: 5.64 us -> none
    pallas_call x1 -> x2, Pallas kernels: 46.5 us -> 42.4 us  [the longest x1 41.1 us: body(): pl.pallas_call(kernel, out_shape=[held(cells, ROWS), held(cells, ROWS), h...]
where the time goes in v2:
time: 43.1 us; the launch traced here: 43 us
  Pallas kernels  42.4 us (98%)
  between operations  0.64 us (1%)
    pallas_call x1, Pallas kernels, body(): pl.pallas_call(kernel, out_shape=[held(cells, ROWS), held(cells, ROWS), h...  41.1 us
    pallas_call x1, Pallas kernels, body(): pl.pallas_call(functools.partial(hand_over, 1.0 / math.sqrt(total_cells))...  1.23 us

profile of v2, /device:TPU:1, one launch (start us, length us, event | category | flops | bytes accessed | tf_op | source)
XLA Modules:
  0.0 43.0 jit_solution(8343682831757650819)
XLA Ops:
  0.6 41.1 %shard_map.58 = (f32[1536,128]{1,0:T(8,128)S(1)}, f32[1536,128]{1,0:T(8,128)S(1)}, f32[192,128]{1,0:T(8,128)S(1)}) custom-call(f32[1536,128]{1,0:T(8,128)} %bitcast.4, f32[1536,128]{1,0:T(8,128)} %bitcast.5, f32[9,48,48]{2,1,0:T(8,128)} %w_hbm.1), custom_call_target="tpu_custom_call" | custom-call | flops 1528823808 | bytes 3145728 | tf_op jit(solution)/shard_map/pallas_call | solution.py:356
  41.8 1.2 %shard_map.59 = (f32[1536,128]{1,0:T(8,128)}, f32[1536,128]{1,0:T(8,128)}, f32[9,48,48]{2,1,0:T(8,128)}) custom-call(f32[1536,128]{1,0:T(8,128)S(1)} %get-tuple-element.9.resp, f32[1536,128]{1,0:T(8,128)S(1)} %get-tuple-element.10.gfield, f32[192,128]{1,0:T(8,128)S(1)} %get-tuple-element.11.final), custom_call_target="tpu_custom_call" | custom-call | tf_op jit(solution)/shard_map/pallas_call | solution.py:392

commit v3 on v2

--- a/solution.py
+++ b/solution.py
@@ -12,6 +12,7 @@
 COLS = 32
 ROWS = 128
 PART = 24
+THICK = 16
 MESH = pl.DeviceIdType.MESH
 F32 = jnp.float32
 BF16 = jnp.bfloat16
@@ -43,7 +44,7 @@
 
 def kernel(f_hbm, g_hbm, w_hbm, resp, gfield, final,
            fv, gv, w_ref, z, v, p, q, edge, halo, colout, colin, corner, cornerin,
-           part, got, total, whole, in_sem, hs_sem, hr_sem, as_sem, ar_sem):
+           part, pooled, thick, thin, whole, in_sem, hs_sem, hr_sem, as_sem, ar_sem):
     lon = lax.axis_index("lon")
     lat = lax.axis_index("lat")
     n_lon = lax.axis_size("lon")
@@ -63,15 +64,24 @@
     north = (jnp.where(lat == 0, opposite, lon), jnp.where(lat == 0, 0, lat - 1))
     south = (jnp.where(lat == n_lat - 1, opposite, lon),
              jnp.where(lat == n_lat - 1, n_lat - 1, lat + 1))
-    near = [(dx, dc) for dx in range(4) for dc in range(2) if (dx, dc) != (0, 0)]
-    pool = [place((x + dx) % 4, y, depth, (core + dc) % 2) for dx, dc in near]
-    pool_rank = [((x + dx) % 4) * 2 + (core + dc) % 2 for dx, dc in near]
-    along_y = [place(x, (y + k) % 8, depth, core) for k in range(1, 8)]
-    along_z = [place(x, y, (depth + k) % 8, core) for k in range(1, 8)]
     rank = x * 2 + core
 
+    def others(own):
+        return [k + jnp.where(own <= k, 1, 0) for k in range(7)]
+
+    first_is_y = core == 0
+    seats = (jnp.where(first_is_y, y, depth), jnp.where(first_is_y, depth, y))
+
+    def along(way, seat):
+        by_y = first_is_y if way == 0 else jnp.logical_not(first_is_y)
+        return place(x, jnp.where(by_y, seat, y), jnp.where(by_y, depth, seat), core)
+
+    def pool(seat):
+        return place(seat // 2, y, depth, seat % 2)
+
     barrier = pltpu.get_barrier_semaphore()
-    partners = [west, east, north, south] + pool + along_y + along_z
+    partners = [west, east, north, south] + [pool(k) for k in others(rank)]
+    partners += [along(way, k) for way in range(2) for k in others(seats[way])]
     for to in partners:
         pl.semaphore_signal(barrier, inc=1, device_id=to, device_id_type=MESH)
     load_f = pltpu.make_async_copy(f_hbm, fv, in_sem.at[0])
@@ -224,54 +234,68 @@
     part[3 * CH:] = (tail[:CH] + pltpu.roll(tail[CH:2 * CH], 16, 1)
                      + pltpu.roll(tail[2 * CH:], 32, 1))
 
-    def reduce_scatter(k):
-        return remote(part.at[pl.ds(pl.multiple_of(pool_rank[k] * PART, 8), PART)],
-                      got.at[0, k], as_sem.at[0, k], ar_sem.at[0, k], pool[k])
-
-    def exchange(phase, k, to, spot):
-        return remote(total.at[phase - 1], got.at[phase, spot], as_sem.at[phase, k], ar_sem.at[phase, k], to)
-
-    def share(phase):
-        seat = seats[phase]
-        got[phase, seat] = total[phase - 1]
-        for k in range(7):
-            exchange(phase, k, (along_y, along_z)[phase - 1][k], seat).start()
-
-    def gather(k):
-        return remote(total.at[2], whole.at[here], as_sem.at[3, k], ar_sem.at[3, k], pool[k])
-
-    def arrive(phase):
-        for k in range(7):
-            if phase == 0:
-                reduce_scatter(k).wait_recv()
-            else:
-                to = (along_y, along_z)[phase - 1][k]
-                exchange(phase, k, to, (seats[phase] + 7 - k) % 8).wait_recv()
-        value = part[here] if phase == 0 else got[phase, 7]
-        for k in range(7):
-            value = value + got[phase, k]
-        total[phase] = value
-
-    here = pl.ds(pl.multiple_of(rank * PART, 8), PART)
-    seats = [None, y, depth]
+    def chunk(seat):
+        return pl.ds(pl.multiple_of(seat * PART, 8), PART)
+
+    def scatter(to):
+        return remote(part.at[chunk(to)], pooled.at[rank], as_sem.at[0, to], ar_sem.at[0, rank], pool(to))
+
+    def exchange(slots, stage, way, to):
+        own = slots.at[stage - 1, seats[way]]
+        line = 2 * stage - 1 if slots is thick else 2 * stage
+        return remote(own, own, as_sem.at[line, to], ar_sem.at[line, seats[way]], along(way, to))
+
+    def exchanged(slots, stage, way, by):
+        line = 2 * stage - 1 if slots is thick else 2 * stage
+        spot = slots.at[stage - 1, by]
+        return remote(spot, spot, as_sem.at[line, by], ar_sem.at[line, by], along(way, by))
+
+    def gather(to):
+        return remote(whole.at[chunk(rank)], whole.at[chunk(rank)], as_sem.at[5, to], ar_sem.at[5, rank], pool(to))
+
+    def total(slots):
+        value = slots[0]
+        for k in range(1, 8):
+            value = value + slots[k]
+        return value
+
+    def share(stage, thick_value, thin_value):
+        ways = (0, 1) if stage == 1 else (1, 0)
+        thick[stage - 1, seats[ways[0]]] = thick_value
+        thin[stage - 1, seats[ways[1]]] = thin_value
+        for slots, way in zip((thick, thin), ways):
+            for to in others(seats[way]):
+                exchange(slots, stage, way, to).start()
+
+    def collect(stage):
+        ways = (0, 1) if stage == 1 else (1, 0)
+        for slots, way in zip((thick, thin), ways):
+            for by in others(seats[way]):
+                exchanged(slots, stage, way, by).wait_recv()
+        return total(thick.at[stage - 1]), total(thin.at[stage - 1])
+
     corners_out = [
         remote(corner, cornerin.at[1], hs_sem.at[4], hr_sem.at[5], west),
         remote(corner, cornerin.at[0], hs_sem.at[5], hr_sem.at[4], east),
     ]
-    for k in range(7):
-        reduce_scatter(k).start()
+    for to in others(rank):
+        scatter(to).start()
+    pooled[rank] = part[chunk(rank)]
     for copy in corners_out:
         copy.start()
 
     products(p, z, fwd_hi, fwd_lo)
-    products(q, v, adj_hi, adj_lo)
+    product(p, z, fwd_hi, fwd_lo, 0, COLS + 1)
+
+    for by in others(rank):
+        remote(pooled.at[by], pooled.at[by], as_sem.at[0, by], ar_sem.at[0, by], pool(by)).wait_recv()
+    sums = total(pooled)
+    share(1, sums[:THICK], sums[THICK:])
+
     build(v, 0, colin[0, CH:])
     build(v, COLS + 1, colin[1, CH:])
-    product(p, z, fwd_hi, fwd_lo, 0, COLS + 1)
+    products(q, v, adj_hi, adj_lo)
     product(q, v, adj_hi, adj_lo, 0, COLS + 1)
-
-    arrive(0)
-    share(1)
 
     remote(corner, cornerin.at[1], hs_sem.at[4], hr_sem.at[5], west).wait_recv()
     remote(corner, cornerin.at[0], hs_sem.at[5], hr_sem.at[4], east).wait_recv()
@@ -300,28 +324,29 @@
         lane < 2, pltpu.roll(from_west, 64, 1), pltpu.roll(from_east, 64, 1)))
     finish(resp, p, forward[:, :CH], forward[:, 2 * CH:], ring_f)
 
-    arrive(1)
-    share(2)
+    share(2, *collect(1))
+
     low_side, high_side = adjoint[:, :CH], adjoint[:, 2 * CH:]
     ring_g = jnp.where(middle, pltpu.roll(beyond, 64, 1), jnp.where(lane < 2, from_west, from_east))
     finish(gfield, q, jnp.where(lat == 0, high_side, low_side),
            jnp.where(lat == n_lat - 1, low_side, high_side), ring_g)
 
-    arrive(2)
-    for k in range(7):
-        gather(k).start()
-    whole[here] = total[2]
-    for k in range(7):
-        peer = pl.ds(pl.multiple_of((((x + 4 - near[k][0]) % 4) * 2 + (core + near[k][1]) % 2) * PART, 8), PART)
-        remote(total.at[2], whole.at[peer], as_sem.at[3, k], ar_sem.at[3, k], pool[k]).wait_recv()
+    whole[chunk(rank)] = jnp.concatenate(collect(2), axis=0)
+    for to in others(rank):
+        gather(to).start()
+    for by in others(rank):
+        remote(whole.at[chunk(by)], whole.at[chunk(by)], as_sem.at[5, by], ar_sem.at[5, by], pool(by)).wait_recv()
     final[...] = whole[...]
     for copy in halo_out + corners_out:
         copy.wait_send()
-    for k in range(7):
-        reduce_scatter(k).wait_send()
-        exchange(1, k, along_y[k], y).wait_send()
-        exchange(2, k, along_z[k], depth).wait_send()
-        gather(k).wait_send()
+    for to in others(rank):
+        scatter(to).wait_send()
+        gather(to).wait_send()
+    for stage in (1, 2):
+        ways = (0, 1) if stage == 1 else (1, 0)
+        for slots, way in zip((thick, thin), ways):
+            for to in others(seats[way]):
+                exchange(slots, stage, way, to).wait_send()
 
 
 def hand_over(scale, resp, gfield, final, resp_hbm, gfield_hbm, gw_hbm, gw, sem):
@@ -373,14 +398,15 @@
             pltpu.VMEM((CH, ROWS), F32),
             pltpu.VMEM((2, CH, ROWS), F32),
             pltpu.VMEM((8 * PART, ROWS), F32),
-            pltpu.VMEM((3, 8, PART, ROWS), F32),
-            pltpu.VMEM((3, PART, ROWS), F32),
+            pltpu.VMEM((8, PART, ROWS), F32),
+            pltpu.VMEM((2, 8, THICK, ROWS), F32),
+            pltpu.VMEM((2, 8, PART - THICK, ROWS), F32),
             pltpu.VMEM((8 * PART, ROWS), F32),
             pltpu.SemaphoreType.DMA((3,)),
             pltpu.SemaphoreType.DMA((6,)),
             pltpu.SemaphoreType.DMA((6,)),
-            pltpu.SemaphoreType.DMA((4, 7)),
-            pltpu.SemaphoreType.DMA((4, 7)),
+            pltpu.SemaphoreType.DMA((6, 8)),
+            pltpu.SemaphoreType.DMA((6, 8)),
         ],
         compiler_params=pltpu.CompilerParams(
             collective_id=0, has_side_effects=True, vmem_limit_bytes=40 << 20

time: 43.1 us -> 40.7 us (0.944)
  Pallas kernels: 42.4 us -> 39.9 us
    pallas_call x1, Pallas kernels: 41.1 us -> 38.7 us  [body(): pl.pallas_call(kernel, out_shape=[held(cells, ROWS), held(cells, ROWS), h...]
where the time goes in v3:
time: 40.7 us; the launch traced here: 40.6 us
  Pallas kernels  39.9 us (98%)
  between operations  0.64 us (2%)
    pallas_call x1, Pallas kernels, body(): pl.pallas_call(kernel, out_shape=[held(cells, ROWS), held(cells, ROWS), h...  38.7 us
    pallas_call x1, Pallas kernels, body(): pl.pallas_call(functools.partial(hand_over, 1.0 / math.sqrt(total_cells))...  1.23 us

profile of v3, /device:TPU:1, one launch (start us, length us, event | category | flops | bytes accessed | tf_op | source)
XLA Modules:
  0.0 40.6 jit_solution(11220982446726347777)
XLA Ops:
  0.6 38.7 %shard_map.58 = (f32[1536,128]{1,0:T(8,128)S(1)}, f32[1536,128]{1,0:T(8,128)S(1)}, f32[192,128]{1,0:T(8,128)S(1)}) custom-call(f32[1536,128]{1,0:T(8,128)} %bitcast.4, f32[1536,128]{1,0:T(8,128)} %bitcast.5, f32[9,48,48]{2,1,0:T(8,128)} %w_hbm.1), custom_call_target="tpu_custom_call" | custom-call | flops 1528823808 | bytes 3145728 | tf_op jit(solution)/shard_map/pallas_call | solution.py:381
  39.3 1.2 %shard_map.59 = (f32[1536,128]{1,0:T(8,128)}, f32[1536,128]{1,0:T(8,128)}, f32[9,48,48]{2,1,0:T(8,128)}) custom-call(f32[1536,128]{1,0:T(8,128)S(1)} %get-tuple-element.9.resp, f32[1536,128]{1,0:T(8,128)S(1)} %get-tuple-element.10.gfield, f32[192,128]{1,0:T(8,128)S(1)} %get-tuple-element.11.final), custom_call_target="tpu_custom_call" | custom-call | tf_op jit(solution)/shard_map/pallas_call | solution.py:418

commit v4 on v3

--- a/solution.py
+++ b/solution.py
@@ -82,26 +82,27 @@
     barrier = pltpu.get_barrier_semaphore()
     partners = [west, east, north, south] + [pool(k) for k in others(rank)]
     partners += [along(way, k) for way in range(2) for k in others(seats[way])]
-    for to in partners:
-        pl.semaphore_signal(barrier, inc=1, device_id=to, device_id_type=MESH)
     load_f = pltpu.make_async_copy(f_hbm, fv, in_sem.at[0])
     load_g = pltpu.make_async_copy(g_hbm, gv, in_sem.at[1])
     load_w = pltpu.make_async_copy(w_hbm, w_ref, in_sem.at[2])
     load_f.start()
     load_g.start()
     load_w.start()
+    for to in partners:
+        pl.semaphore_signal(barrier, inc=1, device_id=to, device_id_type=MESH)
     v[0] = jnp.zeros((6 * CH, ROWS), BF16)
     v[COLS + 1] = jnp.zeros((6 * CH, ROWS), BF16)
+    lane = lax.broadcasted_iota(jnp.int32, (CH, ROWS), 1)
+
+    def pack(src, base, acc):
+        def step(j, acc):
+            return jnp.where(lane // 2 == j + base // 2, pltpu.roll(column(src, j), (2 * j + base + 1) % 128, 1), acc)
+        return lax.fori_loop(0, COLS, step, acc, unroll=16)
+
     load_f.wait()
+    packed_f = pack(fv, 0, jnp.zeros((CH, ROWS), F32))
     load_g.wait()
-
-    lane = lax.broadcasted_iota(jnp.int32, (CH, ROWS), 1)
-
-    def pack(j, acc):
-        acc = jnp.where(lane // 2 == j, pltpu.roll(column(fv, j), 2 * j + 1, 1), acc)
-        return jnp.where(lane // 2 == j + 32, pltpu.roll(column(gv, j), (2 * j + 65) % 128, 1), acc)
-
-    edge[...] = lax.fori_loop(0, COLS, pack, jnp.zeros((CH, ROWS), F32), unroll=8)
+    edge[...] = pack(gv, 64, packed_f)
     for side, j in enumerate((0, COLS - 1)):
         colout[side, :CH] = column(fv, j)
         colout[side, CH:] = column(gv, j)
@@ -127,10 +128,10 @@
     from_north = jnp.where(lat == 0, 0, 1)
     from_south = jnp.where(lat == n_lat - 1, 1, 0)
     halo_out = [
+        remote(colout.at[0], colin.at[1], hs_sem.at[2], hr_sem.at[3], west),
+        remote(colout.at[1], colin.at[0], hs_sem.at[3], hr_sem.at[2], east),
         remote(edge, halo.at[from_north], hs_sem.at[0], hr_sem.at[from_north], north),
         remote(edge, halo.at[from_south], hs_sem.at[1], hr_sem.at[from_south], south),
-        remote(colout.at[0], colin.at[1], hs_sem.at[2], hr_sem.at[3], west),
-        remote(colout.at[1], colin.at[0], hs_sem.at[3], hr_sem.at[2], east),
     ]
     for copy in halo_out:
         copy.start()
@@ -263,9 +264,16 @@
         ways = (0, 1) if stage == 1 else (1, 0)
         thick[stage - 1, seats[ways[0]]] = thick_value
         thin[stage - 1, seats[ways[1]]] = thin_value
+        lines = [[(slots, way, to) for to in others(seats[way])] for slots, way in zip((thick, thin), ways)]
+        for pair in zip(*lines):
+            for slots, way, to in pair:
+                exchange(slots, stage, way, to).start()
+
+    def settle(stage):
+        ways = (0, 1) if stage == 1 else (1, 0)
         for slots, way in zip((thick, thin), ways):
             for to in others(seats[way]):
-                exchange(slots, stage, way, to).start()
+                exchange(slots, stage, way, to).wait_send()
 
     def collect(stage):
         ways = (0, 1) if stage == 1 else (1, 0)
@@ -324,6 +332,10 @@
         lane < 2, pltpu.roll(from_west, 64, 1), pltpu.roll(from_east, 64, 1)))
     finish(resp, p, forward[:, :CH], forward[:, 2 * CH:], ring_f)
 
+    for copy in halo_out + corners_out:
+        copy.wait_send()
+    for to in others(rank):
+        scatter(to).wait_send()
     share(2, *collect(1))
 
     low_side, high_side = adjoint[:, :CH], adjoint[:, 2 * CH:]
@@ -331,22 +343,16 @@
     finish(gfield, q, jnp.where(lat == 0, high_side, low_side),
            jnp.where(lat == n_lat - 1, low_side, high_side), ring_g)
 
+    settle(1)
     whole[chunk(rank)] = jnp.concatenate(collect(2), axis=0)
     for to in others(rank):
         gather(to).start()
+    settle(2)
     for by in others(rank):
         remote(whole.at[chunk(by)], whole.at[chunk(by)], as_sem.at[5, by], ar_sem.at[5, by], pool(by)).wait_recv()
     final[...] = whole[...]
-    for copy in halo_out + corners_out:
-        copy.wait_send()
     for to in others(rank):
-        scatter(to).wait_send()
         gather(to).wait_send()
-    for stage in (1, 2):
-        ways = (0, 1) if stage == 1 else (1, 0)
-        for slots, way in zip((thick, thin), ways):
-            for to in others(seats[way]):
-                exchange(slots, stage, way, to).wait_send()
 
 
 def hand_over(scale, resp, gfield, final, resp_hbm, gfield_hbm, gw_hbm, gw, sem):

time: 40.7 us -> 40.3 us (level)
  no operation moved by 1% of the time
where the time goes in v4:
time: 40.3 us; the launch traced here: 40.2 us
  Pallas kernels  39.5 us (98%)
  between operations  0.64 us (2%)
    pallas_call x1, Pallas kernels, body(): pl.pallas_call(kernel, out_shape=[held(cells, ROWS), held(cells, ROWS), h...  38.3 us
    pallas_call x1, Pallas kernels, body(): pl.pallas_call(functools.partial(hand_over, 1.0 / math.sqrt(total_cells))...  1.23 us

profile of v4, /device:TPU:1, one launch (start us, length us, event | category | flops | bytes accessed | tf_op | source)
XLA Modules:
  0.0 40.2 jit_solution(4143749799220417153)
XLA Ops:
  0.6 38.3 %shard_map.58 = (f32[1536,128]{1,0:T(8,128)S(1)}, f32[1536,128]{1,0:T(8,128)S(1)}, f32[192,128]{1,0:T(8,128)S(1)}) custom-call(f32[1536,128]{1,0:T(8,128)} %bitcast.4, f32[1536,128]{1,0:T(8,128)} %bitcast.5, f32[9,48,48]{2,1,0:T(8,128)} %w_hbm.1), custom_call_target="tpu_custom_call" | custom-call | flops 1528823808 | bytes 3145728 | tf_op jit(solution)/shard_map/pallas_call | solution.py:387
  38.9 1.2 %shard_map.59 = (f32[1536,128]{1,0:T(8,128)}, f32[1536,128]{1,0:T(8,128)}, f32[9,48,48]{2,1,0:T(8,128)}) custom-call(f32[1536,128]{1,0:T(8,128)S(1)} %get-tuple-element.9.resp, f32[1536,128]{1,0:T(8,128)S(1)} %get-tuple-element.10.gfield, f32[192,128]{1,0:T(8,128)S(1)} %get-tuple-element.11.final), custom_call_target="tpu_custom_call" | custom-call | tf_op jit(solution)/shard_map/pallas_call | solution.py:424

commit v5 on v4

--- a/solution.py
+++ b/solution.py
@@ -44,7 +44,7 @@
 
 def kernel(f_hbm, g_hbm, w_hbm, resp, gfield, final,
            fv, gv, w_ref, z, v, p, q, edge, halo, colout, colin, corner, cornerin,
-           part, pooled, thick, thin, whole, in_sem, hs_sem, hr_sem, as_sem, ar_sem):
+           part, pooled, thick, thin, in_sem, hs_sem, hr_sem, as_sem, ar_sem):
     lon = lax.axis_index("lon")
     lat = lax.axis_index("lat")
     n_lon = lax.axis_size("lon")
@@ -231,9 +231,6 @@
     acc = acc + dot_nt(jnp.concatenate(left_rows, axis=0), jnp.concatenate(right_rows, axis=0))
 
     part[:3 * CH] = acc[:, :128]
-    tail = jnp.concatenate([acc[:, 128:], jnp.zeros((3 * CH, 112), F32)], axis=1)
-    part[3 * CH:] = (tail[:CH] + pltpu.roll(tail[CH:2 * CH], 16, 1)
-                     + pltpu.roll(tail[2 * CH:], 32, 1))
 
     def chunk(seat):
         return pl.ds(pl.multiple_of(seat * PART, 8), PART)
@@ -252,7 +249,7 @@
         return remote(spot, spot, as_sem.at[line, by], ar_sem.at[line, by], along(way, by))
 
     def gather(to):
-        return remote(whole.at[chunk(rank)], whole.at[chunk(rank)], as_sem.at[5, to], ar_sem.at[5, rank], pool(to))
+        return remote(final.at[chunk(rank)], final.at[chunk(rank)], as_sem.at[5, to], ar_sem.at[5, rank], pool(to))
 
     def total(slots):
         value = slots[0]
@@ -286,7 +283,12 @@
         remote(corner, cornerin.at[1], hs_sem.at[4], hr_sem.at[5], west),
         remote(corner, cornerin.at[0], hs_sem.at[5], hr_sem.at[4], east),
     ]
-    for to in others(rank):
+    for to in others(rank)[:5]:
+        scatter(to).start()
+    tail = jnp.concatenate([acc[:, 128:], jnp.zeros((3 * CH, 112), F32)], axis=1)
+    part[3 * CH:] = (tail[:CH] + pltpu.roll(tail[CH:2 * CH], 16, 1)
+                     + pltpu.roll(tail[2 * CH:], 32, 1))
+    for to in others(rank)[5:]:
         scatter(to).start()
     pooled[rank] = part[chunk(rank)]
     for copy in corners_out:
@@ -344,13 +346,12 @@
            jnp.where(lat == n_lat - 1, low_side, high_side), ring_g)
 
     settle(1)
-    whole[chunk(rank)] = jnp.concatenate(collect(2), axis=0)
+    final[chunk(rank)] = jnp.concatenate(collect(2), axis=0)
     for to in others(rank):
         gather(to).start()
     settle(2)
     for by in others(rank):
-        remote(whole.at[chunk(by)], whole.at[chunk(by)], as_sem.at[5, by], ar_sem.at[5, by], pool(by)).wait_recv()
-    final[...] = whole[...]
+        remote(final.at[chunk(by)], final.at[chunk(by)], as_sem.at[5, by], ar_sem.at[5, by], pool(by)).wait_recv()
     for to in others(rank):
         gather(to).wait_send()
 
@@ -407,7 +408,6 @@
             pltpu.VMEM((8, PART, ROWS), F32),
             pltpu.VMEM((2, 8, THICK, ROWS), F32),
             pltpu.VMEM((2, 8, PART - THICK, ROWS), F32),
-            pltpu.VMEM((8 * PART, ROWS), F32),
             pltpu.SemaphoreType.DMA((3,)),
             pltpu.SemaphoreType.DMA((6,)),
             pltpu.SemaphoreType.DMA((6,)),

time: 40.3 us -> 40.2 us (level)
  no operation moved by 1% of the time
where the time goes in v5:
time: 40.2 us; the launch traced here: 40.1 us
  Pallas kernels  39.5 us (98%)
  between operations  0.64 us (2%)
    pallas_call x1, Pallas kernels, body(): pl.pallas_call(kernel, out_shape=[held(cells, ROWS), held(cells, ROWS), h...  38.2 us
    pallas_call x1, Pallas kernels, body(): pl.pallas_call(functools.partial(hand_over, 1.0 / math.sqrt(total_cells))...  1.23 us

profile of v5, /device:TPU:1, one launch (start us, length us, event | category | flops | bytes accessed | tf_op | source)
XLA Modules:
  0.0 40.1 jit_solution(2850819939375039240)
XLA Ops:
  0.6 38.2 %shard_map.58 = (f32[1536,128]{1,0:T(8,128)S(1)}, f32[1536,128]{1,0:T(8,128)S(1)}, f32[192,128]{1,0:T(8,128)S(1)}) custom-call(f32[1536,128]{1,0:T(8,128)} %bitcast.4, f32[1536,128]{1,0:T(8,128)} %bitcast.5, f32[9,48,48]{2,1,0:T(8,128)} %w_hbm.1), custom_call_target="tpu_custom_call" | custom-call | flops 1528823808 | bytes 3145728 | tf_op jit(solution)/shard_map/pallas_call | solution.py:388
  38.9 1.2 %shard_map.59 = (f32[1536,128]{1,0:T(8,128)}, f32[1536,128]{1,0:T(8,128)}, f32[9,48,48]{2,1,0:T(8,128)}) custom-call(f32[1536,128]{1,0:T(8,128)S(1)} %get-tuple-element.9.resp, f32[1536,128]{1,0:T(8,128)S(1)} %get-tuple-element.10.gfield, f32[192,128]{1,0:T(8,128)S(1)} %get-tuple-element.11.final), custom_call_target="tpu_custom_call" | custom-call | tf_op jit(solution)/shard_map/pallas_call | solution.py:424

commit v6 on v5

--- a/solution.py
+++ b/solution.py
@@ -97,7 +97,7 @@
     def pack(src, base, acc):
         def step(j, acc):
             return jnp.where(lane // 2 == j + base // 2, pltpu.roll(column(src, j), (2 * j + base + 1) % 128, 1), acc)
-        return lax.fori_loop(0, COLS, step, acc, unroll=16)
+        return lax.fori_loop(0, COLS, step, acc, unroll=COLS)
 
     load_f.wait()
     packed_f = pack(fv, 0, jnp.zeros((CH, ROWS), F32))
@@ -216,13 +216,11 @@
         left_rows.append(packed(jnp.where(inside, value, 0.0), True))
     remote(edge, halo.at[0], hs_sem.at[0], hr_sem.at[0], north).wait_recv()
     remote(edge, halo.at[1], hs_sem.at[1], hr_sem.at[1], south).wait_recv()
-    beyond = jnp.where(
+    across = jnp.where(
         lane % 2 == 0,
-        pltpu.roll(halo[1], 1 + is_south, 1),
-        pltpu.roll(halo[0], 3 - is_north, 1),
+        pltpu.roll(halo[1], (127 + is_south) % 128, 1),
+        pltpu.roll(halo[0], 1 - is_north, 1),
     )
-    corner[...] = beyond
-    across = pltpu.roll(beyond, 126, 1)
     right_rows = [
         packed(jnp.where(inside & (lane % 2 == 1), across, 0.0), False),
         jnp.zeros((CH, 256), BF16),
@@ -291,6 +289,8 @@
     for to in others(rank)[5:]:
         scatter(to).start()
     pooled[rank] = part[chunk(rank)]
+    beyond = pltpu.roll(across, 2, 1)
+    corner[...] = beyond
     for copy in corners_out:
         copy.start()
 

time: 40.2 us -> 40.2 us (level)
  no operation moved by 1% of the time
where the time goes in v6:
time: 40.2 us; the launch traced here: 40 us
  Pallas kernels  39.4 us (98%)
  between operations  0.64 us (2%)
    pallas_call x1, Pallas kernels, body(): pl.pallas_call(kernel, out_shape=[held(cells, ROWS), held(cells, ROWS), h...  38.2 us
    pallas_call x1, Pallas kernels, body(): pl.pallas_call(functools.partial(hand_over, 1.0 / math.sqrt(total_cells))...  1.23 us

profile of v6, /device:TPU:1, one launch (start us, length us, event | category | flops | bytes accessed | tf_op | source)
XLA Modules:
  0.0 40.0 jit_solution(16209006282895109312)
XLA Ops:
  0.6 38.2 %shard_map.58 = (f32[1536,128]{1,0:T(8,128)S(1)}, f32[1536,128]{1,0:T(8,128)S(1)}, f32[192,128]{1,0:T(8,128)S(1)}) custom-call(f32[1536,128]{1,0:T(8,128)} %bitcast.4, f32[1536,128]{1,0:T(8,128)} %bitcast.5, f32[9,48,48]{2,1,0:T(8,128)} %w_hbm.1), custom_call_target="tpu_custom_call" | custom-call | flops 1528823808 | bytes 3145728 | tf_op jit(solution)/shard_map/pallas_call | solution.py:388
  38.8 1.2 %shard_map.59 = (f32[1536,128]{1,0:T(8,128)}, f32[1536,128]{1,0:T(8,128)}, f32[9,48,48]{2,1,0:T(8,128)}) custom-call(f32[1536,128]{1,0:T(8,128)S(1)} %get-tuple-element.9.resp, f32[1536,128]{1,0:T(8,128)S(1)} %get-tuple-element.10.gfield, f32[192,128]{1,0:T(8,128)S(1)} %get-tuple-element.11.final), custom_call_target="tpu_custom_call" | custom-call | tf_op jit(solution)/shard_map/pallas_call | solution.py:424
